TPU v7x, 32 devices: a whole 2x2x4 slice. The times are simulated.
32 devices in a mesh: dp: 2 (over x), tp: 4 (over y, core), ep: 4 (over z).
Axes of the slice: x: 2, y: 2, z: 4, core: 2. Of those that a mesh axis runs over, the one named last changes fastest.
Arguments:
- queries: bfloat16 [24, 128, 576], P(('dp', 'ep'), 'tp'), may hold values from -24 to 24
- cache: bfloat16 [192, 128, 576], P(('dp', 'tp', 'ep')), may hold values from -12 to 12
- tables: int32 [32, 6], P(('dp', 'tp', 'ep')), may hold values from 0 to 5, each once within a row
- lengths: int32 [2, 4, 3], P('dp', 'ep'), may hold values from 1 to 1024, 2048 in all within a row
- mig_cache: bfloat16 [64, 128, 576], P(('dp', 'tp', 'ep')), may hold values from -12 to 12
- mig_src: int32 [4], P('ep'), may hold values from 0 to 1
- mig_dst: int32 [4], P('ep'), may hold values from 0 to 1, as said below
- mig_seq: int32 [4], P('ep'), may hold values from 0 to 2
- tokens: bfloat16 [512, 3584], P(('dp', 'tp', 'ep')), may hold values from -6 to 6
- routes: int32 [512, 2], P(('dp', 'tp', 'ep')), may hold values from 0 to 3, all different within a row; in each aligned block of 16 rows (0 to 15, 16 to 31, ...) at most 16 rows name the same one
- gates: float32 [512, 2], P(('dp', 'tp', 'ep')), may hold values from 0.1 to 1
- gate_w: bfloat16 [4, 3584, 2048], P('ep', None, ('dp', 'tp')), may hold values from -0.09375 to 0.09375
- up_w: bfloat16 [4, 3584, 2048], P('ep', None, ('dp', 'tp')), may hold values from -0.09375 to 0.09375
- down_w: bfloat16 [4, 2048, 3584], P('ep', None, ('dp', 'tp')), may hold values from -0.125 to 0.125
Outputs:
- attn_out: bfloat16 [24, 128, 512], P(('dp', 'ep'), 'tp')
- moe_out: bfloat16 [512, 3584], P(('dp', 'tp', 'ep'))
Inputs may be any that keep to these rules, and one draw needn't show every extreme that they name: `tables`: each device's row is an ordering of its 6 page ids. The lengths of each group's 3 requests sum to 2048. `mig_dst`: differs from mig_src at every index. `routes`: each row names 2 different experts; in the rows of one device no expert is named more than 16 times, a bound that some block reaches.
All inputs are finite; a program needn't handle non-finite values.
Results may differ from a plain program's by a relative error of at most 0.0058.
Values may be sent and summed in bfloat16 or wider, within the bound.
A program may use at most 64 MiB of HBM per device.

v0:
```python
import jax
import jax.numpy as jnp
from jax import lax
from jax.sharding import PartitionSpec as P

KV_RANK = 512
ROPE_DIM = 64
PAGE = 128
SLOTS = 2


score_scale = 0.07216878364870322
neg_fill = -1e30


def broadcast(x, axis, root):
    mine = lax.axis_index(axis) == root
    return lax.psum(jnp.where(mine, x, jnp.zeros_like(x)), axis)


def per_device(
    queries,
    cache,
    tables,
    lengths,
    mig_cache,
    mig_src,
    mig_dst,
    mig_seq,
    tokens,
    routes,
    gates,
    gate_w,
    up_w,
    down_w,
):
    tensor_parallel_ranks = lax.axis_size("tp")
    rank_tp = lax.axis_index("tp")
    rank_dp = lax.axis_index("dp")
    row_width = KV_RANK + ROPE_DIM
    group_query = lax.all_gather(queries, "tp", axis=1, tiled=True)
    seqs_group = group_query.shape[0]
    moved_pages = broadcast(mig_cache, "dp", mig_src[0])
    own_pages = cache[tables.reshape(seqs_group, SLOTS)]
    chosen = (rank_dp == mig_dst[0]) & (jnp.arange(seqs_group) == mig_seq[0])
    key_rows = jnp.where(chosen[:, None, None, None], moved_pages[None], own_pages)
    key_rows = key_rows.reshape(seqs_group, SLOTS * PAGE, row_width)
    positions = (
        (jnp.arange(SLOTS)[:, None] * tensor_parallel_ranks + rank_tp) * PAGE
        + jnp.arange(PAGE)[None, :]
    ).reshape(-1)
    valid = positions[None, :] < lengths[0, 0][:, None]
    scores = (
        jnp.einsum("shc,skc->shk", group_query, key_rows, preferred_element_type=jnp.float32)
        * score_scale
    )
    masked = jnp.where(valid[:, None, :], scores, neg_fill)
    part_max = jnp.max(masked, axis=2)
    weights = jnp.where(valid[:, None, :], jnp.exp(masked - part_max[..., None]), 0.0).astype(
        jnp.bfloat16
    )
    part_sum = jnp.sum(weights.astype(jnp.float32), axis=2)
    part_acc = jnp.einsum(
        "shk,skc->shc", weights, key_rows[:, :, :KV_RANK], preferred_element_type=jnp.float32
    )
    most = lax.pmax(part_max, "tp")
    factor = jnp.exp(part_max - most)
    numerator, denominator = (
        lax.psum_scatter(part_acc * factor[..., None], "tp", scatter_dimension=1, tiled=True),
        lax.psum_scatter(part_sum * factor, "tp", scatter_dimension=1, tiled=True),
    )
    attn_out = (numerator / denominator[..., None]).astype(jnp.bfloat16)
    ranks_ep = lax.axis_size("ep")
    token_rows = tokens.shape[0]
    top_routes = routes.shape[1]
    width = tokens.shape[1]
    capacity = min(token_rows, max(2, 2 * token_rows * top_routes // ranks_ep))
    slots_all = ranks_ep * capacity
    flattened_index_list = routes.reshape(-1)
    matches = (flattened_index_list[:, None] == jnp.arange(ranks_ep)[None, :]).astype(jnp.int32)
    before = jnp.cumsum(matches, axis=0) - matches
    column = flattened_index_list * capacity + jnp.sum(before * matches, axis=1)
    places = (column[:, None] == jnp.arange(slots_all)[None, :]).reshape(
        token_rows, top_routes, slots_all
    )
    selected_entries = jnp.any(places, axis=1).astype(jnp.bfloat16)
    dispatched_rows = lax.dot_general(
        selected_entries, tokens, (((0,), (0,)), ((), ())), preferred_element_type=jnp.float32
    )
    dispatched_rows = dispatched_rows.astype(jnp.bfloat16).reshape(ranks_ep, capacity, width)
    weight_gate = gate_w[0]
    weight_up = up_w[0]
    weight_down = down_w[0]
    arrived = lax.all_to_all(dispatched_rows, "ep", split_axis=0, concat_axis=0, tiled=True)
    piece = lax.all_gather(arrived[None], ("dp", "tp"), axis=0, tiled=True)
    piece_rows = piece.reshape(-1, width)
    gate = jnp.dot(piece_rows, weight_gate, preferred_element_type=jnp.float32)
    upward = jnp.dot(piece_rows, weight_up, preferred_element_type=jnp.float32)
    hidden_piece = (jax.nn.silu(gate) * upward).astype(jnp.bfloat16)
    hidden = hidden_piece.reshape(piece.shape[:-1] + (weight_gate.shape[1],))
    group_size = hidden.shape[0]
    total_rows = group_size * slots_all
    output_column_slice = weight_down.shape[1]
    summed = jnp.dot(
        lax.all_gather(hidden, ("dp", "tp"), axis=3, tiled=True).reshape(total_rows, -1),
        weight_down,
        preferred_element_type=jnp.float32,
    )
    expert_out = summed.astype(jnp.bfloat16)
    full_rows = lax.all_to_all(
        expert_out.reshape(group_size, slots_all, output_column_slice),
        ("dp", "tp"),
        split_axis=0,
        concat_axis=2,
        tiled=True,
    )
    returned = lax.all_to_all(
        full_rows.reshape(ranks_ep, capacity, width), "ep", split_axis=0, concat_axis=0, tiled=True
    )
    returned_rows = returned.reshape(slots_all, width)
    mixed = jnp.zeros((token_rows, width), jnp.float32)
    for route in range(top_routes):
        chosen_rows = jnp.dot(
            places[:, route].astype(jnp.bfloat16), returned_rows, preferred_element_type=jnp.float32
        )
        mixed = mixed + gates[:, route : route + 1] * chosen_rows
    return (attn_out, mixed.astype(jnp.bfloat16))


def solution(mesh):
    in_specs = (
        P(("dp", "ep"), "tp", None),
        P(("dp", "tp", "ep"), None, None),
        P(("dp", "tp", "ep"), None),
        P("dp", "ep", None),
        P(("dp", "tp", "ep"), None, None),
        P("ep"),
        P("ep"),
        P("ep"),
        P(("dp", "tp", "ep"), None),
        P(("dp", "tp", "ep"), None),
        P(("dp", "tp", "ep"), None),
        P("ep", None, ("dp", "tp")),
        P("ep", None, ("dp", "tp")),
        P("ep", None, ("dp", "tp")),
    )
    out_specs = (P(("dp", "ep"), "tp", None), P(("dp", "tp", "ep"), None))
    return jax.shard_map(
        per_device, mesh=mesh, in_specs=in_specs, out_specs=out_specs, check_vma=False
    )
```

profile of v0, /device:TPU:0, one launch (start us, length us, event | category | flops | bytes accessed | tf_op | source)
XLA Modules:
  0.0 156.4 jit_solution(16902288940596848301)
XLA Ops:
  8.0 0.0 copy-start
  8.0 0.0 copy-start.2
  8.0 0.0 all-gather.6.cloned.1.call-start
  8.1 0.9 copy.49
  9.0 0.1 eq.49
  9.1 0.1 fusion.20
  9.2 0.1 reduce_window_sum.11
  9.2 0.2 select_reduce_fusion
  9.4 0.1 reduce_sum.22
  9.5 0.1 copy.50
  9.6 0.7 multiply_add_fusion
  10.3 0.1 iota_compare_fusion
  10.3 1.2 convolution_convert_fusion
  11.6 19.3 %all_to_all.25 = bf16[4,16,3584]{2,1,0:T(8,128)(2,1)} all-to-all(bf16[4,16,3584]{2,1,0:T(8,128)(2,1)S(1)} %bitcast.73), channel_id=1, replica_groups=mesh['dp'=2,'tp'=4,'ep'=4] {'ep'}, dimensions={0} | all-to-all | bytes 917504 | tf_op jit(solution)/shard_map/all_to_all | solution.py:94
  30.9 0.0 all-gather.6.cloned.1.call-update
  30.9 0.0 all-reduce.2.cloned.1.call-start
  31.6 0.0 copy-done.2
  31.6 0.8 copy_bitcast_fusion
  32.4 0.0 all-reduce.2.cloned.1.call-update
  32.4 0.0 all-gather.4.cloned.1.call-start
  32.5 35.3 %all-gather.6.cloned.1.call-done = bf16[32,16,3584]{2,1,0:T(8,128)(2,1)} async-done(((bf16[4,16,3584]{2,1,0:T(8,128)(2,1)}), bf16[32,16,3584]{2,1,0:T(8,128)(2,1)}) %all-gather.6.cloned.1.call-update) | async-done | bytes 3670032 | tf_op jit(solution)/shard_map/all_gather | solution.py:95
  67.8 3.9 %fusion.6 = f32[512,256]{1,0:T(8,128)S(1)} fusion(bf16[512,3584]{1,0:T(8,128)(2,1)} %bitcast.78, bf16[1,3584,256]{2,1,0:T(8,128)(2,1)} %param.25), kind=kOutput, calls=%fused_computation.10 | convolution fusion | flops 939524096 | bytes 6029312 | tf_op jit(solution)/shard_map/dot_general | solution.py:97
  71.6 0.0 copy-done.6
  71.6 0.4 copy-done.7
  72.0 1.8 %fusion.14 = bf16[512,256]{1,0:T(8,128)(2,1)} fusion(bf16[512,3584]{1,0:T(8,128)(2,1)S(1)} %bitcast.79, bf16[1,3584,256]{2,1,0:T(8,128)(2,1)S(1)} %copy-done.7, f32[512,256]{1,0:T(8,128)S(1)} %fusion.6), kind=kOutput, calls=%fused_computation.15 | convolution fusion | flops 940310528 | bytes 6291456 | tf_op jit(solution)/shard_map/dot_general | solution.py:98
  73.8 0.0 all-gather.4.cloned.1.call-update
  73.9 0.0 reduce-scatter.7.cloned.1.call-start
  75.2 0.5 broadcast.108
  75.7 0.7 reduce.3
  76.4 0.1 reshape.138
  76.5 0.1 reshape.148
  76.6 0.0 copy-start.5
  76.6 1.9 %gather_fusion = bf16[6,128,576]{1,2,0:T(8,128)(2,1)S(1)} fusion(bf16[6,128,576]{1,2,0:T(8,128)(2,1)} %param.15, s32[1024]{0:T(1024)S(1)} %pad_clamp_fusion), kind=kCustom, calls=%fused_computation | custom fusion | bytes 1769496 | tf_op jit(solution)/shard_map/gather | solution.py:44
  78.5 1.3 copy.46
  79.8 10.0 %all_gather.9 = bf16[3,128,576]{2,1,0:T(8,128)(2,1)} all-gather(bf16[3,32,576]{2,1,0:T(8,128)(2,1)S(1)} %copy-done.3), channel_id=1, replica_groups=mesh['dp'=2,'tp'=4,'ep'=4] {'tp'}, dimensions={1}, use_global_device_ids=true | all-gather | bytes 552960 | tf_op jit(solution)/shard_map/all_gather | solution.py:41
  89.8 0.1 add_bitcast_fusion
  89.9 0.1 broadcast_compare_fusion
  90.0 1.2 copy.45
  91.1 1.4 bitcast_select_fusion
  92.6 0.5 fusion.24
  93.0 7.6 %pmax.7 = f32[3,128]{1,0:T(4,128)S(1)} all-reduce(f32[3,128]{1,0:T(4,128)S(1)} %get-tuple-element.8), channel_id=1, replica_groups=mesh['dp'=2,'tp'=4,'ep'=4] {'tp'}, use_global_device_ids=true, to_apply=%region_2.3 | all-reduce | flops 384 | bytes 3072 | tf_op jit(solution)/shard_map/pmax | solution.py:66
  100.6 0.2 convert_reduce_fusion
  100.8 0.7 copy.55
  101.6 0.0 reduce-scatter.7.cloned.1.call-update
  101.6 0.0 reduce-scatter.5.cloned.1.call-start
  101.7 1.4 convolution_multiply_fusion.2
  103.1 0.0 reduce-scatter.5.cloned.1.call-update
  103.1 1.0 all-gather.4.cloned.1.call-done
  104.1 0.0 copy-done
  104.1 2.7 %fusion.8 = bf16[512,448]{0,1:T(8,128)(2,1)S(1)} fusion(bf16[512,2048]{1,0:T(8,128)(2,1)} %bitcast.80, bf16[1,2048,448]{1,2,0:T(8,128)(2,1)S(1)} %copy-done), kind=kOutput, calls=%fused_computation.13 | convolution fusion | flops 939753472 | bytes 4390912 | tf_op jit(solution)/shard_map/dot_general | solution.py:104
  106.8 0.2 copy.51
  107.0 0.0 copy-start.4
  107.1 11.4 %all_to_all.26 = bf16[8,64,448]{2,1,0:T(8,128)(2,1)S(1)} all-to-all(bf16[8,64,448]{2,1,0:T(8,128)(2,1)S(1)} %bitcast.71), channel_id=1, replica_groups=mesh['dp'=2,'tp'=4,'ep'=4] {'dp','tp'}, dimensions={0} | all-to-all | bytes 917504 | tf_op jit(solution)/shard_map/all_to_all | solution.py:110
  118.5 0.3 copy.52
  118.8 1.3 reshape.144
  120.1 4.6 %all-to-all-start.2 = ((bf16[4,16,3584]{2,1,0:T(8,128)(2,1)}), bf16[4,16,3584]{2,1,0:T(8,128)(2,1)S(1)}, u32[]{:S(2)}, u32[]{:S(2)}) async-start(bf16[4,16,3584]{2,1,0:T(8,128)(2,1)} %reshape.144), calls=%async_computation.3 | async-start | bytes 917504 | tf_op jit(solution)/shard_map/all_to_all | solution.py:117
  124.7 0.0 copy-done.4
  124.7 0.0 reduce-scatter.7.cloned.1.call-done
  124.8 0.8 copy.56
  125.6 20.6 %reduce-scatter.5.cloned.1.call-done = f32[3,32,512]{2,1,0:T(8,128)} async-done(((f32[3,128,512]{2,1,0:T(8,128)}), f32[3,32,512]{2,1,0:T(8,128)}) %reduce-scatter.5.cloned.1.call-update) | async-done | bytes 196624 | tf_op jit(solution)/shard_map/reduce_scatter | solution.py:69
  146.2 1.7 %divide_convert_fusion = bf16[3,32,512]{2,1,0:T(8,128)(2,1)} fusion(f32[3,32,512]{2,1,0:T(8,128)} %reduce-scatter.5.cloned.1.call-done, f32[3,32]{1,0:T(4,128)S(1)} %copy.56), kind=kLoop, calls=%fused_computation.25 | loop fusion | flops 98304 | bytes 295296 | tf_op jit(solution)/shard_map/convert_element_type | solution.py:72
  147.8 0.0 all-to-all-done.2
  147.8 0.2 convolution_multiply_fusion.1
  148.0 0.8 fusion.1
  (16 shorter events, 0.1 us)
Async XLA Ops:
  8.0 96.1 %copy-start = (bf16[1,2048,448]{1,2,0:T(8,128)(2,1)S(1)}, bf16[1,2048,448]{1,2,0:T(8,128)(2,1)}, u32[]{:S(2)}) copy-start(bf16[1,2048,448]{1,2,0:T(8,128)(2,1)} %param.27) | copy-start | bytes 5505028
  8.0 23.6 %copy-start.2 = (bf16[2,128,576]{1,2,0:T(8,128)(2,1)S(1)}, bf16[2,128,576]{1,2,0:T(8,128)(2,1)}, u32[]{:S(2)}) copy-start(bf16[2,128,576]{1,2,0:T(8,128)(2,1)} %param.18) | copy-start | bytes 884740
  8.0 59.7 %all-gather.6.cloned.1.call-start = ((), (), s32[]{:S(2)}) async-start(), calls=%async_computation.8 | async-start | bytes 4128768 | tf_op jit(solution)/shard_map/all_gather | solution.py:95
  30.9 59.1 %all-reduce.2.cloned.1.call-start = ((), (), s32[]{:S(2)}) async-start(), calls=%async_computation.5 | async-start | bytes 589824 | tf_op jit(solution)/shard_map/psum | solution.py:18
  32.4 71.7 %all-gather.4.cloned.1.call-start = ((), (), s32[]{:S(2)}) async-start(), calls=%async_computation.7 | async-start | bytes 2359296 | tf_op jit(solution)/shard_map/all_gather | solution.py:105
  67.8 3.9 %copy-start.6 = (bf16[32,16,3584]{2,1,0:T(8,128)(2,1)S(1)}, bf16[32,16,3584]{2,1,0:T(8,128)(2,1)}, u32[]{:S(2)}) copy-start(bf16[32,16,3584]{2,1,0:T(8,128)(2,1)} %all-gather.6.cloned.1.call-done) | copy-start | bytes 11010052
  67.8 4.3 %copy-start.7 = (bf16[1,3584,256]{2,1,0:T(8,128)(2,1)S(1)}, bf16[1,3584,256]{2,1,0:T(8,128)(2,1)}, u32[]{:S(2)}) copy-start(bf16[1,3584,256]{2,1,0:T(8,128)(2,1)} %param.26) | copy-start | bytes 5505028
  72.0 3.7 %copy-start.8 = (s32[1,6]{1,0:T(1,128)S(1)}, s32[1,6]{1,0:T(1,128)}, u32[]{:S(2)}) copy-start(s32[1,6]{1,0:T(1,128)} %param.16) | copy-start | bytes 76
  73.9 50.9 %reduce-scatter.7.cloned.1.call-start = ((), (), s32[]{:S(2)}) async-start(), calls=%async_computation.9 | async-start | bytes 81920
  76.6 3.3 %copy-start.3 = (bf16[3,32,576]{2,1,0:T(8,128)(2,1)S(1)}, bf16[3,32,576]{2,1,0:T(8,128)(2,1)}, u32[]{:S(2)}) copy-start(bf16[3,32,576]{2,1,0:T(8,128)(2,1)} %param.14) | copy-start | bytes 331780
  76.6 13.3 %copy-start.5 = (s32[1,1,3]{2,1,0:T(1,128)S(1)}, s32[1,1,3]{2,1,0:T(1,128)}, u32[]{:S(2)}) copy-start(s32[1,1,3]{2,1,0:T(1,128)} %param.17) | copy-start | bytes 40
  91.1 1.4 copy-start.1
  101.6 44.6 %reduce-scatter.5.cloned.1.call-start = ((), (), s32[]{:S(2)}) async-start(), calls=%async_computation.6 | async-start | bytes 983040 | tf_op jit(solution)/shard_map/reduce_scatter | solution.py:69
  107.0 17.7 %copy-start.4 = (f32[16,2]{0,1:T(2,128)S(1)}, f32[16,2]{0,1:T(2,128)}, u32[]{:S(2)}) copy-start(f32[16,2]{0,1:T(2,128)} %param.24) | copy-start | bytes 388
  120.1 27.7 %all-to-all-start.2 = ((bf16[4,16,3584]{2,1,0:T(8,128)(2,1)}), bf16[4,16,3584]{2,1,0:T(8,128)(2,1)S(1)}, u32[]{:S(2)}, u32[]{:S(2)}) async-start(bf16[4,16,3584]{2,1,0:T(8,128)(2,1)} %reshape.144), calls=%async_computation.3 | async-start | bytes 917504 | tf_op jit(solution)/shard_map/all_to_all | solution.py:117
Sparse Core Ops, SparseCore 0:
  31.0 36.6 all-gather.5
  74.0 30.0 all-gather.3
Sparse Core Ops, SparseCore 1:
  33.6 23.1 all-reduce.1
  101.7 18.7 reduce-scatter.6
  123.0 23.1 reduce-scatter.4
where the time goes:
time: 157 us; the launch traced here: 156 us
  waiting for transfers between devices  57 us (36%)
  blocking collectives  48.3 us (31%)
  between operations  17.8 us (11%)
  matrix products  12.5 us (8%)
  local copies, waits for them, and re-layouts  10 us (6%)
  other arithmetic  5.96 us (4%)
  starting transfers between devices  4.81 us (3%)
    all_gather x1, waiting for transfers between devices, per_device(): piece = lax.all_gather(arrived[None], ('dp', 'tp'), axis=0, tiled=True)  35.3 us
    reduce_scatter x1, waiting for transfers between devices, per_device(): lax.psum_scatter(part_acc * factor[..., None], 'tp', scatter_dimension=1,...  20.6 us
    all_to_all x1, blocking collectives, per_device(): lax.all_to_all(dispatched_rows, 'ep', split_axis=0, concat_axis=0, tiled=...  19.3 us
    all_to_all x1, blocking collectives, per_device(): lax.all_to_all(expert_out.reshape(group_size, slots_all, output_column_sl...  11.4 us
    all_gather x1, blocking collectives, per_device(): group_query = lax.all_gather(queries, 'tp', axis=1, tiled=True)  9.96 us
    pmax x1, blocking collectives, per_device(): most = lax.pmax(part_max, 'tp')  7.63 us
    all_to_all x1, starting transfers between devices, per_device(): lax.all_to_all(full_rows.reshape(ranks_ep, capacity, width), 'ep', split_...  4.6 us
    dot_general x1, matrix products, per_device(): gate = jnp.dot(piece_rows, weight_gate, preferred_element_type=jnp.float32)  3.86 us
  transfers between devices with their start and end apart: 6, of which 3 were waited for; matrix products, arithmetic and copies ran while one was open for 15% of the time, Pallas kernels for 0%

commit v1 on v0

--- a/solution.py
+++ b/solution.py
@@ -1,6 +1,8 @@
 import jax
 import jax.numpy as jnp
 from jax import lax
+from jax.experimental import pallas as pl
+from jax.experimental.pallas import tpu as pltpu
 from jax.sharding import PartitionSpec as P
 
 KV_RANK = 512
@@ -127,7 +129,483 @@
     return (attn_out, mixed.astype(jnp.bfloat16))
 
 
+MESH = pl.DeviceIdType.MESH
+PLANE = 8
+LAYERS = 4
+
+
+def window_kernel(
+    tables_ref,
+    lengths_ref,
+    mig_ref,
+    queries_ref,
+    cache_ref,
+    pages_ref,
+    tokens_ref,
+    routes_ref,
+    gates_ref,
+    gate_w_ref,
+    up_w_ref,
+    down_w_ref,
+    attn_ref,
+    moe_ref,
+    tok,
+    hid,
+    out,
+    ret,
+    wg,
+    wu,
+    wd,
+    qry,
+    pool,
+    moved,
+    part,
+    part_in,
+    stat,
+    stat_in,
+    loc_sem,
+    zs,
+    zr,
+    ts,
+    tr,
+    hs,
+    hr,
+    os_,
+    or_,
+    qs,
+    qr,
+    ms,
+    ps,
+    pr,
+    ss,
+    sr,
+):
+    x = lax.axis_index("dp")
+    t = lax.axis_index("tp")
+    z = lax.axis_index("ep")
+    y = lax.div(t, 2)
+    c = lax.rem(t, 2)
+    me = x * 4 + t
+    ax, ay = lax.rem(x + 1 + c, 2), lax.rem(y + c, 2)
+    bx, by = lax.rem(x + c, 2), lax.rem(y + 1 + c, 2)
+    at, bt, st = ay * 2 + c, by * 2 + c, y * 2 + (1 - c)
+    dev_a, dev_b, dev_s = (ax, at, z), (bx, bt, z), (x, st, z)
+    dt = (1 - y) * 2 + c
+    id_a, id_b, id_d = ax * 4 + at, bx * 4 + bt, (1 - x) * 4 + dt
+    flip = 1 - 2 * c
+    z_pair = lax.div(z, 2) * 2 + lax.rem(z + 1, 2)
+    inner = lax.div(z + 1, 2) == 1
+
+    def layer(i):
+        return lax.rem(lax.div(z, 2) + lax.div(i, 2), 2) * 2 + lax.rem(z + i, 2)
+
+    def remote(src, dst, send, recv, device):
+        return pltpu.make_async_remote_copy(
+            src_ref=src,
+            dst_ref=dst,
+            send_sem=send,
+            recv_sem=recv,
+            device_id=device,
+            device_id_type=MESH,
+        )
+
+    barrier = pltpu.get_barrier_semaphore()
+    world = PLANE * LAYERS
+
+    def greet(j, carry):
+        number = lax.rem(me * LAYERS + z + j, world)
+        pl.semaphore_signal(
+            barrier,
+            inc=1,
+            device_id=(
+                lax.div(number, 16),
+                lax.rem(lax.div(number, LAYERS), 4),
+                lax.rem(number, LAYERS),
+            ),
+            device_id_type=MESH,
+        )
+        return carry
+
+    own_block = tok.at[z, me]
+    local = [
+        pltpu.make_async_copy(tokens_ref, own_block, loc_sem.at[0]),
+        pltpu.make_async_copy(queries_ref, qry.at[t], loc_sem.at[1]),
+        pltpu.make_async_copy(cache_ref, pool, loc_sem.at[2]),
+        pltpu.make_async_copy(gate_w_ref.at[0], wg, loc_sem.at[3]),
+        pltpu.make_async_copy(up_w_ref.at[0], wu, loc_sem.at[4]),
+        pltpu.make_async_copy(down_w_ref.at[0], wd, loc_sem.at[5]),
+    ]
+    for copy in local:
+        copy.start()
+    lax.fori_loop(1, world, greet, 0)
+    pl.semaphore_wait(barrier, world - 1)
+
+    def to_a(buf, k, send, recv):
+        return remote(buf.at[k, me], buf.at[k, me], send.at[k, 0], recv.at[k, 0], dev_a)
+
+    def to_b(buf, k, send, recv):
+        return remote(buf.at[k, me], buf.at[k, me], send.at[k, 1], recv.at[k, 1], dev_b)
+
+    def on_b(buf, k, send, recv):
+        return remote(buf.at[k, id_a], buf.at[k, id_a], send.at[k, 2], recv.at[k, 2], dev_b)
+
+    def to_s(buf, k, send, recv, n, ident):
+        return remote(
+            buf.at[k, ident], buf.at[k, ident], send.at[k, 3 + n], recv.at[k, 3 + n], dev_s
+        )
+
+    def from_s(buf, k, send, recv, n, ident):
+        other = ident + flip
+        return remote(
+            buf.at[k, other], buf.at[k, other], send.at[k, 3 + n], recv.at[k, 3 + n], dev_s
+        )
+
+    def arrived(buf, k, send, recv, n, ident):
+        return remote(buf.at[k, ident], buf.at[k, ident], send.at[k, n], recv.at[k, n], dev_a)
+
+    def cast_start(*group):
+        to_a(*group).start()
+        to_b(*group).start()
+        to_s(*group, 0, me).start()
+
+    def cast_forward(*group):
+        arrived(*group, 0, id_a).wait_recv()
+        on_b(*group).start()
+        to_s(*group, 1, id_a).start()
+        arrived(*group, 1, id_b).wait_recv()
+        to_s(*group, 2, id_b).start()
+
+    def cast_end(*group):
+        arrived(*group, 2, id_d).wait_recv()
+        to_s(*group, 3, id_d).start()
+        for n, ident in enumerate((me, id_b, id_a, id_d)):
+            from_s(*group, n, ident).wait_recv()
+
+    def cast_sent(*group):
+        to_a(*group).wait_send()
+        to_b(*group).wait_send()
+        on_b(*group).wait_send()
+        for n, ident in enumerate((me, id_a, id_b, id_d)):
+            to_s(*group, n, ident).wait_send()
+
+    def tok_group(i):
+        return (tok, layer(i), ts, tr)
+
+    def hid_group(i):
+        return (hid, layer(i), hs, hr)
+
+    def z_copy(k, n, target):
+        return remote(tok.at[k, me], tok.at[k, me], zs.at[k, n], zr.at[k], (x, t, target))
+
+    def out_copy(k, p):
+        return remote(
+            out.at[k, p],
+            ret.at[z, me],
+            os_.at[k, p],
+            or_.at[z, me],
+            (lax.div(p, 4), lax.rem(p, 4), k),
+        )
+
+    def out_send(i):
+        k = layer(i)
+
+        def send(j, carry):
+            out_copy(k, lax.rem(me + j, PLANE)).start()
+            return carry
+
+        lax.fori_loop(lax.div(3 - i, 3), PLANE, send, 0)
+
+    local[0].wait()
+    z_copy(z, 0, z_pair).start()
+
+    @pl.when(inner)
+    def _():
+        z_copy(z, 1, 3 - z).start()
+
+    y_dev, x_dev = (x, dt, z), (1 - x, t, z)
+    local[1].wait()
+    q_far = remote(qry.at[t], qry.at[t], qs.at[0], qr.at[0], y_dev)
+    q_near = remote(qry.at[t], qry.at[t], qs.at[1], qr.at[1], dev_s)
+    q_far.start()
+    q_near.start()
+    cast_start(*tok_group(0))
+    page_copy = remote(pages_ref, moved, ms.at[0], ms.at[1], x_dev)
+    page_copy.start()
+
+    remote(qry.at[dt], qry.at[dt], qs.at[0], qr.at[0], y_dev).wait_recv()
+    q_pass = remote(qry.at[dt], qry.at[dt], qs.at[2], qr.at[2], dev_s)
+    q_pass.start()
+    cast_forward(*tok_group(0))
+    remote(qry.at[st], qry.at[st], qs.at[1], qr.at[1], dev_s).wait_recv()
+    sd = (1 - y) * 2 + (1 - c)
+    remote(qry.at[sd], qry.at[sd], qs.at[2], qr.at[2], dev_s).wait_recv()
+    local[2].wait()
+    page_copy.wait_recv()
+
+    receives = mig_ref[1] == x
+    lane = lax.broadcasted_iota(jnp.int32, (HEADS_ALL, 128), 1)
+    stats = jnp.zeros((HEADS_ALL, 128), jnp.float32)
+    for s in range(3):
+        chosen = receives & (mig_ref[2] == s)
+        query = qry[:, s].reshape(HEADS_ALL, KV_RANK + ROPE_DIM)
+        pages, masked = [], []
+        for j in range(SLOTS):
+            page = jnp.where(chosen, moved[j], pool[tables_ref[0, s * SLOTS + j]])
+            score = (
+                lax.dot_general(
+                    query, page, (((1,), (1,)), ((), ())), preferred_element_type=jnp.float32
+                )
+                * score_scale
+            )
+            position = (j * 4 + t) * PAGE + lax.broadcasted_iota(
+                jnp.int32, (HEADS_ALL, PAGE), 1
+            )
+            valid = position < lengths_ref[0, 0, s]
+            pages.append((page, valid))
+            masked.append(jnp.where(valid, score, neg_fill))
+        top = jnp.max(jnp.maximum(masked[0], masked[1]), axis=1, keepdims=True)
+        total = jnp.zeros((HEADS_ALL, 1), jnp.float32)
+        acc = jnp.zeros((HEADS_ALL, KV_RANK), jnp.float32)
+        for j in range(SLOTS):
+            page, valid = pages[j]
+            weight = jnp.where(valid, jnp.exp(masked[j] - top), 0.0).astype(jnp.bfloat16)
+            total = total + jnp.sum(weight.astype(jnp.float32), axis=1, keepdims=True)
+            acc = acc + jnp.dot(
+                weight, page[:, :KV_RANK], preferred_element_type=jnp.float32
+            )
+        stats = jnp.where(lane == s, top, stats)
+        stats = jnp.where(lane == 3 + s, total, stats)
+        part[:, s] = acc.astype(jnp.bfloat16).reshape(4, HEADS_ALL // 4, KV_RANK)
+    stat[...] = stats.reshape(4, HEADS_ALL // 4, 128)
+
+    def part_copies(j):
+        u = lax.rem(t + j, 4)
+        device = (x, u, z)
+        return (
+            remote(part.at[u], part_in.at[t], ps.at[u], pr.at[t], device),
+            remote(stat.at[u], stat_in.at[t], ss.at[u], sr.at[t], device),
+        )
+
+    for j in range(1, 4):
+        for copy in part_copies(j):
+            copy.start()
+
+    local[3].wait()
+    local[4].wait()
+    local[5].wait()
+
+    def step(i, carry):
+        @pl.when(i < 3)
+        def _():
+            k = layer(i + 1)
+            z_copy(k, 0, z_pair).wait_recv()
+
+            @pl.when(inner)
+            def _():
+                first = lax.div(2 - i, 2)
+                target = first * (3 - z) + (1 - first) * z_pair
+                z_copy(k, 0, target).start()
+
+            cast_start(*tok_group(i + 1))
+
+        @pl.when(i < 4)
+        def _():
+            cast_end(*tok_group(i))
+            k = layer(i)
+            rows = tok[k].reshape(PLANE * 16, tok.shape[3])
+            gate = jnp.dot(rows, wg[...], preferred_element_type=jnp.float32)
+            up = jnp.dot(rows, wu[...], preferred_element_type=jnp.float32)
+            hid[k, me] = (gate / (1.0 + jnp.exp(-gate)) * up).astype(jnp.bfloat16)
+            cast_start(*hid_group(i))
+
+        @pl.when(i < 3)
+        def _():
+            cast_forward(*tok_group(i + 1))
+
+        @pl.when(i < 4)
+        def _():
+            cast_forward(*hid_group(i))
+
+        @pl.when(i > 0)
+        def _():
+            cast_end(*hid_group(i - 1))
+            k = layer(i - 1)
+            depth = hid.shape[3]
+            total = jnp.dot(
+                hid[k, 0], wd[pl.ds(0, depth), :], preferred_element_type=jnp.float32
+            )
+            for p in range(1, PLANE):
+                total = total + jnp.dot(
+                    hid[k, p], wd[pl.ds(p * depth, depth), :], preferred_element_type=jnp.float32
+                )
+            out[k] = total.astype(jnp.bfloat16).reshape(PLANE, 16, out.shape[3])
+            out_send(i - 1)
+
+        return carry
+
+    lax.fori_loop(0, 5, step, 0)
+    keep = pltpu.make_async_copy(out.at[z, me], ret.at[z, me], loc_sem.at[6])
+    keep.start()
+
+    for j in range(1, 4):
+        u = lax.rem(t + j, 4)
+        remote(part.at[u], part_in.at[u], ps.at[u], pr.at[u], dev_s).wait_recv()
+        remote(stat.at[u], stat_in.at[u], ss.at[u], sr.at[u], dev_s).wait_recv()
+    part_in[t] = part[t]
+    stat_in[t] = stat[t]
+    for s in range(3):
+        tops = [stat_in[u, :, s : s + 1] for u in range(4)]
+        sums = [stat_in[u, :, 3 + s : 4 + s] for u in range(4)]
+        most = jnp.maximum(jnp.maximum(tops[0], tops[1]), jnp.maximum(tops[2], tops[3]))
+        numerator = jnp.zeros((HEADS_ALL // 4, KV_RANK), jnp.float32)
+        denominator = jnp.zeros((HEADS_ALL // 4, 1), jnp.float32)
+        for u in range(4):
+            factor = jnp.exp(tops[u] - most)
+            numerator = numerator + factor * part_in[u, s].astype(jnp.float32)
+            denominator = denominator + factor * sums[u]
+        attn_ref[s] = (numerator / denominator).astype(jnp.bfloat16)
+
+    q_far.wait_send()
+    q_near.wait_send()
+    q_pass.wait_send()
+    page_copy.wait_send()
+    for j in range(1, 4):
+        for copy in part_copies(j):
+            copy.wait_send()
+    z_copy(z, 0, z_pair).wait_send()
+
+    @pl.when(inner)
+    def _():
+        z_copy(z, 1, 3 - z).wait_send()
+
+    def drain(i, carry):
+        @pl.when((i > 0) & inner)
+        def _():
+            z_copy(layer(i), 0, z_pair).wait_send()
+
+        cast_sent(*tok_group(i))
+        cast_sent(*hid_group(i))
+        return carry
+
+    lax.fori_loop(0, 4, drain, 0)
+
+    def out_wait(i, carry):
+        k = layer(i)
+
+        def one(j, inside):
+            p = lax.rem(me + j, PLANE)
+            out_copy(k, p).wait_send()
+            remote(out.at[k, p], ret.at[k, p], os_.at[k, p], or_.at[k, p], dev_s).wait_recv()
+            return inside
+
+        return lax.fori_loop(lax.div(3 - i, 3), PLANE, one, carry)
+
+    lax.fori_loop(0, 4, out_wait, 0)
+    keep.wait()
+    named, scale = routes_ref[...], gates_ref[...]
+    coefs = []
+    for e in range(LAYERS):
+        hits = jnp.where(named == e, scale, 0.0)
+        coefs.append(hits[:, 0:1] + hits[:, 1:2])
+    span = out.shape[3]
+    for p in range(PLANE):
+        mixed = coefs[0] * ret[0, p].astype(jnp.float32)
+        for e in range(1, LAYERS):
+            mixed = mixed + coefs[e] * ret[e, p].astype(jnp.float32)
+        moe_ref[:, p * span : (p + 1) * span] = mixed.astype(jnp.bfloat16)
+
+
+HEADS_ALL = 128
+
+
+def window(
+    queries,
+    cache,
+    tables,
+    lengths,
+    mig_cache,
+    mig_src,
+    mig_dst,
+    mig_seq,
+    tokens,
+    routes,
+    gates,
+    gate_w,
+    up_w,
+    down_w,
+):
+    mig = jnp.concatenate([mig_src, mig_dst, mig_seq])
+    rows, width = tokens.shape
+    depth, span, units = gate_w.shape[2], down_w.shape[2], down_w.shape[1]
+    heads, row_width = queries.shape[1], queries.shape[2]
+    bf16, f32 = jnp.bfloat16, jnp.float32
+    dma = pltpu.SemaphoreType.DMA
+    smem = pl.BlockSpec(memory_space=pltpu.SMEM)
+    vmem = pl.BlockSpec(memory_space=pltpu.VMEM)
+    hbm = pl.BlockSpec(memory_space=pl.ANY)
+    return pl.pallas_call(
+        window_kernel,
+        out_shape=(
+            jax.ShapeDtypeStruct((queries.shape[0], heads, KV_RANK), bf16),
+            jax.ShapeDtypeStruct((rows, width), bf16),
+        ),
+        in_specs=[smem] * 3 + [hbm] * 4 + [vmem] * 2 + [hbm] * 3,
+        out_specs=(vmem, vmem),
+        scratch_shapes=[
+            pltpu.VMEM((LAYERS, PLANE, rows, width), bf16),
+            pltpu.VMEM((LAYERS, PLANE, PLANE * rows, depth), bf16),
+            pltpu.VMEM((LAYERS, PLANE, rows, span), bf16),
+            pltpu.VMEM((LAYERS, PLANE, rows, span), bf16),
+            pltpu.VMEM((width, depth), bf16),
+            pltpu.VMEM((width, depth), bf16),
+            pltpu.VMEM((units, span), bf16),
+            pltpu.VMEM((4, 3, heads, row_width), bf16),
+            pltpu.VMEM(cache.shape, bf16),
+            pltpu.VMEM(mig_cache.shape, bf16),
+            pltpu.VMEM((4, 3, heads, KV_RANK), bf16),
+            pltpu.VMEM((4, 3, heads, KV_RANK), bf16),
+            pltpu.VMEM((4, heads, 128), f32),
+            pltpu.VMEM((4, heads, 128), f32),
+            dma((7,)),
+            dma((4, 2)),
+            dma((4,)),
+            dma((4, 7)),
+            dma((4, 7)),
+            dma((4, 7)),
+            dma((4, 7)),
+            dma((4, PLANE)),
+            dma((4, PLANE)),
+            dma((3,)),
+            dma((3,)),
+            dma((2,)),
+            dma((4,)),
+            dma((4,)),
+            dma((4,)),
+            dma((4,)),
+        ],
+        compiler_params=pltpu.CompilerParams(
+            collective_id=0, has_side_effects=True, vmem_limit_bytes=48 * 1024 * 1024
+        ),
+    )(
+        tables,
+        lengths,
+        mig,
+        queries,
+        cache,
+        mig_cache,
+        tokens,
+        routes,
+        gates,
+        gate_w,
+        up_w,
+        down_w,
+    )
+
+
 def solution(mesh):
+    form = per_device
+    if (mesh.shape["dp"], mesh.shape["tp"], mesh.shape["ep"]) == (2, 4, LAYERS):
+        form = window
     in_specs = (
         P(("dp", "ep"), "tp", None),
         P(("dp", "tp", "ep"), None, None),
@@ -146,5 +624,5 @@
     )
     out_specs = (P(("dp", "ep"), "tp", None), P(("dp", "tp", "ep"), None))
     return jax.shard_map(
-        per_device, mesh=mesh, in_specs=in_specs, out_specs=out_specs, check_vma=False
-    )
+        form, mesh=mesh, in_specs=in_specs, out_specs=out_specs, check_vma=False
+    )

time: 157 us -> 93.1 us (0.59)
  Pallas kernels: 0 us -> 79.1 us
  waiting for transfers between devices: 57 us -> 0 us
  blocking collectives: 48.3 us -> 0 us
  between operations: 17.8 us -> 2.66 us
  matrix products: 12.5 us -> 0 us
  other arithmetic: 5.96 us -> 0.08 us
  starting transfers between devices: 4.81 us -> 0 us
    pallas_call x0 -> x1, Pallas kernels: none -> 79.1 us  [window(): pl.pallas_call(window_kernel, out_shape=(jax.ShapeDtypeStruct((queries.sh...]
    all_gather x2 -> x0, waiting for transfers between devices: 36.3 us -> none  [the longest x1 35.3 us: per_device(): piece = lax.all_gather(arrived[None], ('dp', 'tp'), axis=0, tiled=True)]
    all_to_all x2 -> x0, blocking collectives: 30.7 us -> none  [the longest x1 19.3 us: per_device(): lax.all_to_all(dispatched_rows, 'ep', split_axis=0, concat_axis=0, tiled=...]
    reduce_scatter x1 -> x0, waiting for transfers between devices: 20.6 us -> none  [per_device(): lax.psum_scatter(part_acc * factor[..., None], 'tp', scatter_dimension=1,...]
    dot_general x8 -> x0, matrix products: 12.5 us -> none  [the longest x1 3.86 us: per_device(): gate = jnp.dot(piece_rows, weight_gate, preferred_element_type=jnp.float32)]
    all_gather x1 -> x0, blocking collectives: 9.96 us -> none  [per_device(): group_query = lax.all_gather(queries, 'tp', axis=1, tiled=True)]
    pmax x1 -> x0, blocking collectives: 7.63 us -> none  [per_device(): most = lax.pmax(part_max, 'tp')]
    unnamed x22 -> x19, local copies, waits for them, and re-layouts: 3.39 us -> 11 us
  transfers between devices with their start and end apart: 6 -> 0, of which waited for: 3 -> 0; matrix products, arithmetic and copies ran while one was open for 15% -> 0% of each run, Pallas kernels for 0% -> 0%
where the time goes in v1:
time: 93.1 us; the launch traced here: 92.8 us
  Pallas kernels  79.1 us (85%)
  local copies, waits for them, and re-layouts  11 us (12%)
  between operations  2.66 us (3%)
    pallas_call x1, Pallas kernels, window(): pl.pallas_call(window_kernel, out_shape=(jax.ShapeDtypeStruct((queries.sh...  79.1 us
    unnamed x19, local copies, waits for them, and re-layouts  11 us

profile of v1, /device:TPU:0, one launch (start us, length us, event | category | flops | bytes accessed | tf_op | source)
XLA Modules:
  0.0 92.8 jit_solution(6715722756916873853)
XLA Ops:
  2.6 0.1 pad_add_fusion.mig_ref
  2.6 0.8 copy.18.routes_ref
  3.4 0.8 copy.19.gates_ref
  4.2 1.2 %copy.17.pages_ref = bf16[2,128,576]{2,1,0:T(8,128)(2,1)S(1)} copy(bf16[2,128,576]{1,2,0:T(8,128)(2,1)} %param.18) | data formatting | bytes 589824 | tf_op args[4]
  5.3 1.5 %copy.16.cache_ref = bf16[6,128,576]{2,1,0:T(8,128)(2,1)S(1)} copy(bf16[6,128,576]{1,2,0:T(8,128)(2,1)} %param.15) | data formatting | bytes 1769472 | tf_op args[1]
  6.9 0.0 copy-start
  6.9 0.0 copy-start.2
  6.9 0.0 copy-start.3
  6.9 0.0 copy-start.4
  6.9 0.0 copy-start.5
  6.9 4.0 %copy.20.down_w_ref = bf16[1,2048,448]{2,1,0:T(8,128)(2,1)} copy(bf16[1,2048,448]{1,2,0:T(8,128)(2,1)} %param.27) | data formatting | bytes 3670016 | tf_op args[13]
  10.9 0.0 copy-done
  10.9 0.0 copy-done.2
  10.9 0.0 copy-done.3
  10.9 0.0 copy-done.4
  10.9 0.0 copy-done.5
  10.9 0.0 copy-start.1
  10.9 1.5 %copy-done.1 = bf16[1,3584,256]{2,1,0:T(8,128)(2,1)S(1)} copy-done((bf16[1,3584,256]{2,1,0:T(8,128)(2,1)S(1)}, bf16[1,3584,256]{2,1,0:T(8,128)(2,1)}, u32[]{:S(2)}) %copy-start.1) | copy-done | bytes 1835032
  12.4 79.1 %shard_map.149 = (bf16[3,32,512]{2,1,0:T(8,128)(2,1)S(1)}, bf16[16,3584]{1,0:T(8,128)(2,1)S(1)}) custom-call(s32[1,6]{1,0:T(1,128)S(1)} %copy-done.4, s32[1,1,3]{2,1,0:T(1,128)S(1)} %copy-done.5, s32[3]{0:T(128)S(1)} %pad_add_fusion.mig_ref, bf16[3,32,576]{2,1,0:T(8,128)(2,1)S(1)} %copy-done.2, bf16[6,128,576]{2,1,0:T(8,128)(2,1)S(1)} %copy.16.cache_ref, ...), custom_call_target="tpu_custom_call" | custom-call | tf_op jit(solution)/shard_map/pallas_call | solution.py:546
  91.5 0.6 copy.26
  92.2 0.6 copy.27
Async XLA Ops:
  6.9 4.0 %copy-start = (bf16[1,3584,256]{2,1,0:T(8,128)(2,1)S(1)}, bf16[1,3584,256]{2,1,0:T(8,128)(2,1)}, u32[]{:S(2)}) copy-start(bf16[1,3584,256]{2,1,0:T(8,128)(2,1)} %gate_w_ref.1) | copy-start | bytes 5505028
  6.9 4.0 %copy-start.2 = (bf16[3,32,576]{2,1,0:T(8,128)(2,1)S(1)}, bf16[3,32,576]{2,1,0:T(8,128)(2,1)}, u32[]{:S(2)}) copy-start(bf16[3,32,576]{2,1,0:T(8,128)(2,1)} %queries_ref.1) | copy-start | bytes 331780
  6.9 4.0 %copy-start.3 = (bf16[16,3584]{1,0:T(8,128)(2,1)S(1)}, bf16[16,3584]{1,0:T(8,128)(2,1)}, u32[]{:S(2)}) copy-start(bf16[16,3584]{1,0:T(8,128)(2,1)} %tokens_ref.1) | copy-start | bytes 344068
  6.9 4.0 %copy-start.4 = (s32[1,6]{1,0:T(1,128)S(1)}, s32[1,6]{1,0:T(1,128)}, u32[]{:S(2)}) copy-start(s32[1,6]{1,0:T(1,128)} %tables_ref.1) | copy-start | bytes 76
  6.9 4.0 %copy-start.5 = (s32[1,1,3]{2,1,0:T(1,128)S(1)}, s32[1,1,3]{2,1,0:T(1,128)}, u32[]{:S(2)}) copy-start(s32[1,1,3]{2,1,0:T(1,128)} %lengths_ref.1) | copy-start | bytes 40
  10.9 1.5 %copy-start.1 = (bf16[1,3584,256]{2,1,0:T(8,128)(2,1)S(1)}, bf16[1,3584,256]{2,1,0:T(8,128)(2,1)}, u32[]{:S(2)}) copy-start(bf16[1,3584,256]{2,1,0:T(8,128)(2,1)} %up_w_ref.1) | copy-start | bytes 5505028

commit v2 on v1

--- a/solution.py
+++ b/solution.py
@@ -328,55 +328,9 @@
     q_near = remote(qry.at[t], qry.at[t], qs.at[1], qr.at[1], dev_s)
     q_far.start()
     q_near.start()
-    cast_start(*tok_group(0))
     page_copy = remote(pages_ref, moved, ms.at[0], ms.at[1], x_dev)
-    page_copy.start()
-
-    remote(qry.at[dt], qry.at[dt], qs.at[0], qr.at[0], y_dev).wait_recv()
     q_pass = remote(qry.at[dt], qry.at[dt], qs.at[2], qr.at[2], dev_s)
-    q_pass.start()
-    cast_forward(*tok_group(0))
-    remote(qry.at[st], qry.at[st], qs.at[1], qr.at[1], dev_s).wait_recv()
     sd = (1 - y) * 2 + (1 - c)
-    remote(qry.at[sd], qry.at[sd], qs.at[2], qr.at[2], dev_s).wait_recv()
-    local[2].wait()
-    page_copy.wait_recv()
-
-    receives = mig_ref[1] == x
-    lane = lax.broadcasted_iota(jnp.int32, (HEADS_ALL, 128), 1)
-    stats = jnp.zeros((HEADS_ALL, 128), jnp.float32)
-    for s in range(3):
-        chosen = receives & (mig_ref[2] == s)
-        query = qry[:, s].reshape(HEADS_ALL, KV_RANK + ROPE_DIM)
-        pages, masked = [], []
-        for j in range(SLOTS):
-            page = jnp.where(chosen, moved[j], pool[tables_ref[0, s * SLOTS + j]])
-            score = (
-                lax.dot_general(
-                    query, page, (((1,), (1,)), ((), ())), preferred_element_type=jnp.float32
-                )
-                * score_scale
-            )
-            position = (j * 4 + t) * PAGE + lax.broadcasted_iota(
-                jnp.int32, (HEADS_ALL, PAGE), 1
-            )
-            valid = position < lengths_ref[0, 0, s]
-            pages.append((page, valid))
-            masked.append(jnp.where(valid, score, neg_fill))
-        top = jnp.max(jnp.maximum(masked[0], masked[1]), axis=1, keepdims=True)
-        total = jnp.zeros((HEADS_ALL, 1), jnp.float32)
-        acc = jnp.zeros((HEADS_ALL, KV_RANK), jnp.float32)
-        for j in range(SLOTS):
-            page, valid = pages[j]
-            weight = jnp.where(valid, jnp.exp(masked[j] - top), 0.0).astype(jnp.bfloat16)
-            total = total + jnp.sum(weight.astype(jnp.float32), axis=1, keepdims=True)
-            acc = acc + jnp.dot(
-                weight, page[:, :KV_RANK], preferred_element_type=jnp.float32
-            )
-        stats = jnp.where(lane == s, top, stats)
-        stats = jnp.where(lane == 3 + s, total, stats)
-        part[:, s] = acc.astype(jnp.bfloat16).reshape(4, HEADS_ALL // 4, KV_RANK)
-    stat[...] = stats.reshape(4, HEADS_ALL // 4, 128)
 
     def part_copies(j):
         u = lax.rem(t + j, 4)
@@ -386,64 +340,127 @@
             remote(stat.at[u], stat_in.at[t], ss.at[u], sr.at[t], device),
         )
 
-    for j in range(1, 4):
-        for copy in part_copies(j):
-            copy.start()
-
-    local[3].wait()
-    local[4].wait()
-    local[5].wait()
+    def attend():
+        remote(qry.at[st], qry.at[st], qs.at[1], qr.at[1], dev_s).wait_recv()
+        remote(qry.at[sd], qry.at[sd], qs.at[2], qr.at[2], dev_s).wait_recv()
+        local[2].wait()
+        page_copy.wait_recv()
+        receives = mig_ref[1] == x
+        lane = lax.broadcasted_iota(jnp.int32, (HEADS_ALL, 128), 1)
+        stats = jnp.zeros((HEADS_ALL, 128), jnp.float32)
+        for s in range(3):
+            chosen = receives & (mig_ref[2] == s)
+            query = qry[:, s].reshape(HEADS_ALL, KV_RANK + ROPE_DIM)
+            pages, masked = [], []
+            for j in range(SLOTS):
+                page = jnp.where(chosen, moved[j], pool[tables_ref[0, s * SLOTS + j]])
+                score = (
+                    lax.dot_general(
+                        query, page, (((1,), (0,)), ((), ())), preferred_element_type=jnp.float32
+                    )
+                    * score_scale
+                )
+                position = (j * 4 + t) * PAGE + lax.broadcasted_iota(
+                    jnp.int32, (HEADS_ALL, PAGE), 1
+                )
+                valid = position < lengths_ref[0, 0, s]
+                pages.append((page, valid))
+                masked.append(jnp.where(valid, score, neg_fill))
+            top = jnp.max(jnp.maximum(masked[0], masked[1]), axis=1, keepdims=True)
+            total = jnp.zeros((HEADS_ALL, 1), jnp.float32)
+            acc = jnp.zeros((HEADS_ALL, KV_RANK), jnp.float32)
+            for j in range(SLOTS):
+                page, valid = pages[j]
+                weight = jnp.where(valid, jnp.exp(masked[j] - top), 0.0).astype(jnp.bfloat16)
+                total = total + jnp.sum(weight.astype(jnp.float32), axis=1, keepdims=True)
+                acc = acc + lax.dot_general(
+                    weight,
+                    page[:KV_RANK],
+                    (((1,), (1,)), ((), ())),
+                    preferred_element_type=jnp.float32,
+                )
+            stats = jnp.where(lane == s, top, stats)
+            stats = jnp.where(lane == 3 + s, total, stats)
+            part[:, s] = acc.astype(jnp.bfloat16).reshape(4, HEADS_ALL // 4, KV_RANK)
+        stat[...] = stats.reshape(4, HEADS_ALL // 4, 128)
+        for j in range(1, 4):
+            for copy in part_copies(j):
+                copy.start()
 
     def step(i, carry):
-        @pl.when(i < 3)
-        def _():
-            k = layer(i + 1)
+        @pl.when(i == 0)
+        def _():
+            cast_start(*tok_group(0))
+
+        @pl.when((i > 0) & (i < 4))
+        def _():
+            k = layer(i)
             z_copy(k, 0, z_pair).wait_recv()
 
             @pl.when(inner)
             def _():
-                first = lax.div(2 - i, 2)
+                first = lax.div(3 - i, 2)
                 target = first * (3 - z) + (1 - first) * z_pair
                 z_copy(k, 0, target).start()
 
-            cast_start(*tok_group(i + 1))
-
-        @pl.when(i < 4)
-        def _():
-            cast_end(*tok_group(i))
-            k = layer(i)
+            cast_start(*tok_group(i))
+
+        @pl.when((i > 0) & (i < 5))
+        def _():
+            cast_forward(*tok_group(i - 1))
+
+        @pl.when(i == 1)
+        def _():
+            remote(qry.at[dt], qry.at[dt], qs.at[0], qr.at[0], y_dev).wait_recv()
+            q_pass.start()
+
+        @pl.when(i == 3)
+        def _():
+            page_copy.start()
+
+        @pl.when(i == 2)
+        def _():
+            local[3].wait()
+            local[4].wait()
+            local[5].wait()
+
+        @pl.when((i > 1) & (i < 6))
+        def _():
+            cast_end(*tok_group(i - 2))
+            k = layer(i - 2)
             rows = tok[k].reshape(PLANE * 16, tok.shape[3])
             gate = jnp.dot(rows, wg[...], preferred_element_type=jnp.float32)
             up = jnp.dot(rows, wu[...], preferred_element_type=jnp.float32)
             hid[k, me] = (gate / (1.0 + jnp.exp(-gate)) * up).astype(jnp.bfloat16)
-            cast_start(*hid_group(i))
-
-        @pl.when(i < 3)
-        def _():
-            cast_forward(*tok_group(i + 1))
-
-        @pl.when(i < 4)
-        def _():
-            cast_forward(*hid_group(i))
-
-        @pl.when(i > 0)
-        def _():
-            cast_end(*hid_group(i - 1))
-            k = layer(i - 1)
+            cast_start(*hid_group(i - 2))
+
+        @pl.when(i == 6)
+        def _():
+            attend()
+
+        @pl.when((i > 2) & (i < 7))
+        def _():
+            cast_forward(*hid_group(i - 3))
+
+        @pl.when(i > 3)
+        def _():
+            cast_end(*hid_group(i - 4))
+            k = layer(i - 4)
             depth = hid.shape[3]
-            total = jnp.dot(
-                hid[k, 0], wd[pl.ds(0, depth), :], preferred_element_type=jnp.float32
-            )
-            for p in range(1, PLANE):
-                total = total + jnp.dot(
-                    hid[k, p], wd[pl.ds(p * depth, depth), :], preferred_element_type=jnp.float32
+            total = jnp.zeros((PLANE * 16, out.shape[3]), jnp.float32)
+            for p in range(PLANE):
+                total = total + lax.dot_general(
+                    hid[k, p],
+                    wd[:, p * depth : (p + 1) * depth],
+                    (((1,), (1,)), ((), ())),
+                    preferred_element_type=jnp.float32,
                 )
             out[k] = total.astype(jnp.bfloat16).reshape(PLANE, 16, out.shape[3])
-            out_send(i - 1)
+            out_send(i - 4)
 
         return carry
 
-    lax.fori_loop(0, 5, step, 0)
+    lax.fori_loop(0, 8, step, 0)
     keep = pltpu.make_async_copy(out.at[z, me], ret.at[z, me], loc_sem.at[6])
     keep.start()
 
@@ -503,10 +520,14 @@
     lax.fori_loop(0, 4, out_wait, 0)
     keep.wait()
     named, scale = routes_ref[...], gates_ref[...]
+    count = named.shape[1]
+    same = lax.broadcasted_iota(jnp.int32, (count, count), 0) == lax.broadcasted_iota(
+        jnp.int32, (count, count), 1
+    )
     coefs = []
     for e in range(LAYERS):
-        hits = jnp.where(named == e, scale, 0.0)
-        coefs.append(hits[:, 0:1] + hits[:, 1:2])
+        hits = jnp.sum(jnp.where(named == e, scale, 0.0), axis=0, keepdims=True)
+        coefs.append(jnp.sum(jnp.where(same, hits, 0.0), axis=1, keepdims=True))
     span = out.shape[3]
     for p in range(PLANE):
         mixed = coefs[0] * ret[0, p].astype(jnp.float32)
@@ -538,6 +559,7 @@
     rows, width = tokens.shape
     depth, span, units = gate_w.shape[2], down_w.shape[2], down_w.shape[1]
     heads, row_width = queries.shape[1], queries.shape[2]
+    pool, moved = jnp.swapaxes(cache, 1, 2), jnp.swapaxes(mig_cache, 1, 2)
     bf16, f32 = jnp.bfloat16, jnp.float32
     dma = pltpu.SemaphoreType.DMA
     smem = pl.BlockSpec(memory_space=pltpu.SMEM)
@@ -558,10 +580,10 @@
             pltpu.VMEM((LAYERS, PLANE, rows, span), bf16),
             pltpu.VMEM((width, depth), bf16),
             pltpu.VMEM((width, depth), bf16),
-            pltpu.VMEM((units, span), bf16),
+            pltpu.VMEM((span, units), bf16),
             pltpu.VMEM((4, 3, heads, row_width), bf16),
-            pltpu.VMEM(cache.shape, bf16),
-            pltpu.VMEM(mig_cache.shape, bf16),
+            pltpu.VMEM(pool.shape, bf16),
+            pltpu.VMEM(moved.shape, bf16),
             pltpu.VMEM((4, 3, heads, KV_RANK), bf16),
             pltpu.VMEM((4, 3, heads, KV_RANK), bf16),
             pltpu.VMEM((4, heads, 128), f32),
@@ -584,21 +606,21 @@
             dma((4,)),
         ],
         compiler_params=pltpu.CompilerParams(
-            collective_id=0, has_side_effects=True, vmem_limit_bytes=48 * 1024 * 1024
+            collective_id=0, has_side_effects=True, vmem_limit_bytes=60 * 1024 * 1024
         ),
     )(
         tables,
         lengths,
         mig,
         queries,
-        cache,
-        mig_cache,
+        pool,
+        moved,
         tokens,
-        routes,
-        gates,
+        routes.T,
+        gates.T,
         gate_w,
         up_w,
-        down_w,
+        jnp.swapaxes(down_w, 1, 2),
     )
 
 

time: 93.1 us -> 75.1 us (0.81)
  Pallas kernels: 79.1 us -> 68.7 us
  local copies, waits for them, and re-layouts: 11 us -> 3.09 us
    pallas_call x1, Pallas kernels: 79.1 us -> 68.7 us  [window(): pl.pallas_call(window_kernel, out_shape=(jax.ShapeDtypeStruct((queries.sh...]
    unnamed x19 -> x2, local copies, waits for them, and re-layouts: 11 us -> 3.09 us
where the time goes in v2:
time: 75.1 us; the launch traced here: 74.9 us
  Pallas kernels  68.7 us (91%)
  local copies, waits for them, and re-layouts  3.09 us (4%)
  between operations  2.58 us (3%)
    pallas_call x1, Pallas kernels, window(): pl.pallas_call(window_kernel, out_shape=(jax.ShapeDtypeStruct((queries.sh...  68.7 us
    unnamed x2, local copies, waits for them, and re-layouts  3.09 us

profile of v2, /device:TPU:0, one launch (start us, length us, event | category | flops | bytes accessed | tf_op | source)
XLA Modules:
  0.0 74.9 jit_solution(10209664581398820578)
XLA Ops:
  2.6 0.6 pad_add_fusion.mig_ref
  3.2 68.7 %shard_map.149 = (bf16[3,32,512]{2,1,0:T(8,128)(2,1)}, bf16[16,3584]{1,0:T(8,128)(2,1)}) custom-call(s32[1,6]{1,0:T(1,128)} %tables_ref.1, s32[1,1,3]{2,1,0:T(1,128)} %lengths_ref.1, s32[3]{0:T(128)} %pad_add_fusion.mig_ref, bf16[3,32,576]{2,1,0:T(8,128)(2,1)} %queries_ref.1, bf16[6,576,128]{2,1,0:T(8,128)(2,1)} %bitcast.6, bf16[2,576,128]{2,1,0:T(8,128)(2,1)} %bitcast.7, ...), custom_call_target="tpu_custom_call" | custom-call | tf_op jit(solution)/shard_map/pallas_call | solution.py:568
  71.8 1.5 %copy.21 = bf16[3,32,512]{2,1,0:T(8,128)(2,1)} copy(bf16[3,32,512]{2,1,0:T(8,128)(2,1)} %get-tuple-element.4) | data formatting | bytes 196608
  73.4 1.6 %copy.22 = bf16[16,3584]{1,0:T(8,128)(2,1)} copy(bf16[16,3584]{1,0:T(8,128)(2,1)} %get-tuple-element.5) | data formatting | bytes 229376

commit v3 on v2

--- a/solution.py
+++ b/solution.py
@@ -1,3 +1,5 @@
+import functools
+
 import jax
 import jax.numpy as jnp
 from jax import lax
@@ -196,8 +198,13 @@
     z_pair = lax.div(z, 2) * 2 + lax.rem(z + 1, 2)
     inner = lax.div(z + 1, 2) == 1
 
+    half = lax.div(z, 2)
+
     def layer(i):
-        return lax.rem(lax.div(z, 2) + lax.div(i, 2), 2) * 2 + lax.rem(z + i, 2)
+        first, last = lax.div(3 - i, 3), lax.div(i, 3)
+        middle = 1 - first - last
+        other = (2 - i) * (2 - half) + (i - 1) * (3 - 3 * half)
+        return first * z + middle * other + last * z_pair
 
     def remote(src, dst, send, recv, device):
         return pltpu.make_async_remote_copy(
@@ -263,14 +270,21 @@
     def arrived(buf, k, send, recv, n, ident):
         return remote(buf.at[k, ident], buf.at[k, ident], send.at[k, n], recv.at[k, n], dev_a)
 
-    def cast_start(*group):
-        to_a(*group).start()
-        to_b(*group).start()
+    def cast_start(*group, plane=True):
+        @pl.when(plane)
+        def _():
+            to_a(*group).start()
+            to_b(*group).start()
+
         to_s(*group, 0, me).start()
 
-    def cast_forward(*group):
+    def cast_forward(*group, plane=True):
         arrived(*group, 0, id_a).wait_recv()
-        on_b(*group).start()
+
+        @pl.when(plane)
+        def _():
+            on_b(*group).start()
+
         to_s(*group, 1, id_a).start()
         arrived(*group, 1, id_b).wait_recv()
         to_s(*group, 2, id_b).start()
@@ -296,6 +310,11 @@
 
     def z_copy(k, n, target):
         return remote(tok.at[k, me], tok.at[k, me], zs.at[k, n], zr.at[k], (x, t, target))
+
+    def pair_copy(n, ident):
+        return remote(
+            tok.at[z, ident], tok.at[z, ident], ts.at[z_pair, n], tr.at[z, n], (x, t, z_pair)
+        )
 
     def out_copy(k, p):
         return remote(
@@ -332,13 +351,38 @@
     q_pass = remote(qry.at[dt], qry.at[dt], qs.at[2], qr.at[2], dev_s)
     sd = (1 - y) * 2 + (1 - c)
 
-    def part_copies(j):
-        u = lax.rem(t + j, 4)
-        device = (x, u, z)
+    def part_copies(n):
+        u = (st, sd, dt)[n]
+        device = (dev_s, dev_s, y_dev)[n]
         return (
-            remote(part.at[u], part_in.at[t], ps.at[u], pr.at[t], device),
-            remote(stat.at[u], stat_in.at[t], ss.at[u], sr.at[t], device),
+            remote(part.at[u], part_in.at[n], ps.at[n], pr.at[n], device),
+            remote(stat.at[u], stat_in.at[n], ss.at[n], sr.at[n], device),
         )
+
+    def merge(mine, slots):
+        tops = [stat[mine, :, 0:3]] + [stat_in[n, :, 0:3] for n in slots]
+        sums = [stat[mine, :, 3:6]] + [stat_in[n, :, 3:6] for n in slots]
+        most = functools.reduce(jnp.maximum, tops)
+        factors = [jnp.exp(top - most) for top in tops]
+        denominator = sum(f * a for f, a in zip(factors, sums))
+        numerators = []
+        for s in range(3):
+            value = factors[0][:, s : s + 1] * part[mine, s].astype(jnp.float32)
+            for factor, n in zip(factors[1:], slots):
+                value = value + factor[:, s : s + 1] * part_in[n, s].astype(jnp.float32)
+            numerators.append(value)
+        return most, denominator, numerators
+
+    def pass_on():
+        for copy in part_copies(1):
+            copy.wait_recv()
+        most, denominator, numerators = merge(dt, (1,))
+        stat[dt, :, 0:3] = most
+        stat[dt, :, 3:6] = denominator
+        for s in range(3):
+            part[dt, s] = numerators[s].astype(jnp.bfloat16)
+        for copy in part_copies(2):
+            copy.start()
 
     def attend():
         remote(qry.at[st], qry.at[st], qs.at[1], qr.at[1], dev_s).wait_recv()
@@ -383,8 +427,8 @@
             stats = jnp.where(lane == 3 + s, total, stats)
             part[:, s] = acc.astype(jnp.bfloat16).reshape(4, HEADS_ALL // 4, KV_RANK)
         stat[...] = stats.reshape(4, HEADS_ALL // 4, 128)
-        for j in range(1, 4):
-            for copy in part_copies(j):
+        for n in (1, 0):
+            for copy in part_copies(n):
                 copy.start()
 
     def step(i, carry):
@@ -395,19 +439,28 @@
         @pl.when((i > 0) & (i < 4))
         def _():
             k = layer(i)
-            z_copy(k, 0, z_pair).wait_recv()
-
-            @pl.when(inner)
+
+            @pl.when(i < 3)
             def _():
-                first = lax.div(3 - i, 2)
-                target = first * (3 - z) + (1 - first) * z_pair
-                z_copy(k, 0, target).start()
-
-            cast_start(*tok_group(i))
+                z_copy(k, 0, z_pair).wait_recv()
+
+                @pl.when(inner)
+                def _():
+                    z_copy(k, 0, z_pair).start()
+
+            @pl.when(i == 1)
+            def _():
+                z_copy(z_pair, 0, z_pair).wait_recv()
+
+                @pl.when(inner)
+                def _():
+                    z_copy(z_pair, 0, 3 - z).start()
+
+            cast_start(*tok_group(i), plane=i < 3)
 
         @pl.when((i > 0) & (i < 5))
         def _():
-            cast_forward(*tok_group(i - 1))
+            cast_forward(*tok_group(i - 1), plane=i < 4)
 
         @pl.when(i == 1)
         def _():
@@ -427,6 +480,12 @@
         @pl.when((i > 1) & (i < 6))
         def _():
             cast_end(*tok_group(i - 2))
+
+            @pl.when(i == 2)
+            def _():
+                for n, ident in enumerate((id_a, id_b, id_d)):
+                    pair_copy(n, ident).start()
+
             k = layer(i - 2)
             rows = tok[k].reshape(PLANE * 16, tok.shape[3])
             gate = jnp.dot(rows, wg[...], preferred_element_type=jnp.float32)
@@ -437,6 +496,10 @@
         @pl.when(i == 6)
         def _():
             attend()
+
+        @pl.when(i == 7)
+        def _():
+            pass_on()
 
         @pl.when((i > 2) & (i < 7))
         def _():
@@ -464,30 +527,19 @@
     keep = pltpu.make_async_copy(out.at[z, me], ret.at[z, me], loc_sem.at[6])
     keep.start()
 
-    for j in range(1, 4):
-        u = lax.rem(t + j, 4)
-        remote(part.at[u], part_in.at[u], ps.at[u], pr.at[u], dev_s).wait_recv()
-        remote(stat.at[u], stat_in.at[u], ss.at[u], sr.at[u], dev_s).wait_recv()
-    part_in[t] = part[t]
-    stat_in[t] = stat[t]
+    for n in (0, 2):
+        for copy in part_copies(n):
+            copy.wait_recv()
+    most, denominator, numerators = merge(t, (0, 2))
     for s in range(3):
-        tops = [stat_in[u, :, s : s + 1] for u in range(4)]
-        sums = [stat_in[u, :, 3 + s : 4 + s] for u in range(4)]
-        most = jnp.maximum(jnp.maximum(tops[0], tops[1]), jnp.maximum(tops[2], tops[3]))
-        numerator = jnp.zeros((HEADS_ALL // 4, KV_RANK), jnp.float32)
-        denominator = jnp.zeros((HEADS_ALL // 4, 1), jnp.float32)
-        for u in range(4):
-            factor = jnp.exp(tops[u] - most)
-            numerator = numerator + factor * part_in[u, s].astype(jnp.float32)
-            denominator = denominator + factor * sums[u]
-        attn_ref[s] = (numerator / denominator).astype(jnp.bfloat16)
+        attn_ref[s] = (numerators[s] / denominator[:, s : s + 1]).astype(jnp.bfloat16)
 
     q_far.wait_send()
     q_near.wait_send()
     q_pass.wait_send()
     page_copy.wait_send()
-    for j in range(1, 4):
-        for copy in part_copies(j):
+    for n in range(3):
+        for copy in part_copies(n):
             copy.wait_send()
     z_copy(z, 0, z_pair).wait_send()
 
@@ -585,9 +637,9 @@
             pltpu.VMEM(pool.shape, bf16),
             pltpu.VMEM(moved.shape, bf16),
             pltpu.VMEM((4, 3, heads, KV_RANK), bf16),
-            pltpu.VMEM((4, 3, heads, KV_RANK), bf16),
+            pltpu.VMEM((3, 3, heads, KV_RANK), bf16),
             pltpu.VMEM((4, heads, 128), f32),
-            pltpu.VMEM((4, heads, 128), f32),
+            pltpu.VMEM((3, heads, 128), f32),
             dma((7,)),
             dma((4, 2)),
             dma((4,)),
@@ -600,13 +652,13 @@
             dma((3,)),
             dma((3,)),
             dma((2,)),
-            dma((4,)),
-            dma((4,)),
-            dma((4,)),
-            dma((4,)),
+            dma((3,)),
+            dma((3,)),
+            dma((3,)),
+            dma((3,)),
         ],
         compiler_params=pltpu.CompilerParams(
-            collective_id=0, has_side_effects=True, vmem_limit_bytes=60 * 1024 * 1024
+            collective_id=0, has_side_effects=True, vmem_limit_bytes=58 * 1024 * 1024
         ),
     )(
         tables,

time: 75.1 us -> 64.3 us (0.86)
  Pallas kernels: 68.7 us -> 57.8 us
    pallas_call x1, Pallas kernels: 68.7 us -> 57.8 us  [window(): pl.pallas_call(window_kernel, out_shape=(jax.ShapeDtypeStruct((queries.sh...]
where the time goes in v3:
time: 64.3 us; the launch traced here: 64 us
  Pallas kernels  57.8 us (90%)
  local copies, waits for them, and re-layouts  3.09 us (5%)
  between operations  2.58 us (4%)
    pallas_call x1, Pallas kernels, window(): pl.pallas_call(window_kernel, out_shape=(jax.ShapeDtypeStruct((queries.sh...  57.8 us
    unnamed x2, local copies, waits for them, and re-layouts  3.09 us

profile of v3, /device:TPU:0, one launch (start us, length us, event | category | flops | bytes accessed | tf_op | source)
XLA Modules:
  0.0 64.0 jit_solution(17551723254452148928)
XLA Ops:
  2.6 0.6 pad_add_fusion.mig_ref
  3.2 57.8 %shard_map.149 = (bf16[3,32,512]{2,1,0:T(8,128)(2,1)}, bf16[16,3584]{1,0:T(8,128)(2,1)}) custom-call(s32[1,6]{1,0:T(1,128)} %tables_ref.1, s32[1,1,3]{2,1,0:T(1,128)} %lengths_ref.1, s32[3]{0:T(128)} %pad_add_fusion.mig_ref, bf16[3,32,576]{2,1,0:T(8,128)(2,1)} %queries_ref.1, bf16[6,576,128]{2,1,0:T(8,128)(2,1)} %bitcast.6, bf16[2,576,128]{2,1,0:T(8,128)(2,1)} %bitcast.7, ...), custom_call_target="tpu_custom_call" | custom-call | tf_op jit(solution)/shard_map/pallas_call | solution.py:620
  60.9 1.5 %copy.21 = bf16[3,32,512]{2,1,0:T(8,128)(2,1)} copy(bf16[3,32,512]{2,1,0:T(8,128)(2,1)} %get-tuple-element.4) | data formatting | bytes 196608
  62.5 1.6 %copy.22 = bf16[16,3584]{1,0:T(8,128)(2,1)} copy(bf16[16,3584]{1,0:T(8,128)(2,1)} %get-tuple-element.5) | data formatting | bytes 229376

commit v4 on v3

--- a/solution.py
+++ b/solution.py
@@ -139,7 +139,8 @@
 def window_kernel(
     tables_ref,
     lengths_ref,
-    mig_ref,
+    mig_dst_ref,
+    mig_seq_ref,
     queries_ref,
     cache_ref,
     pages_ref,
@@ -197,6 +198,7 @@
     flip = 1 - 2 * c
     z_pair = lax.div(z, 2) * 2 + lax.rem(z + 1, 2)
     inner = lax.div(z + 1, 2) == 1
+    outer = lax.rem(lax.div(z + 1, 2), 2) == 0
 
     half = lax.div(z, 2)
 
@@ -389,11 +391,11 @@
         remote(qry.at[sd], qry.at[sd], qs.at[2], qr.at[2], dev_s).wait_recv()
         local[2].wait()
         page_copy.wait_recv()
-        receives = mig_ref[1] == x
+        receives = mig_dst_ref[0] == x
         lane = lax.broadcasted_iota(jnp.int32, (HEADS_ALL, 128), 1)
         stats = jnp.zeros((HEADS_ALL, 128), jnp.float32)
         for s in range(3):
-            chosen = receives & (mig_ref[2] == s)
+            chosen = receives & (mig_seq_ref[0] == s)
             query = qry[:, s].reshape(HEADS_ALL, KV_RANK + ROPE_DIM)
             pages, masked = [], []
             for j in range(SLOTS):
@@ -440,25 +442,27 @@
         def _():
             k = layer(i)
 
-            @pl.when(i < 3)
+            @pl.when((i < 3) & inner)
             def _():
                 z_copy(k, 0, z_pair).wait_recv()
-
+                z_copy(k, 0, z_pair).start()
+
+            @pl.when(i == 1)
+            def _():
                 @pl.when(inner)
                 def _():
-                    z_copy(k, 0, z_pair).start()
-
-            @pl.when(i == 1)
+                    z_copy(z_pair, 0, z_pair).wait_recv()
+                    z_copy(z_pair, 0, 3 - z).start()
+
+                cast_forward(*tok_group(0))
+
+            @pl.when(outer & (i > 0))
             def _():
-                z_copy(z_pair, 0, z_pair).wait_recv()
-
-                @pl.when(inner)
-                def _():
-                    z_copy(z_pair, 0, 3 - z).start()
+                z_copy(k, 0, z_pair).wait_recv()
 
             cast_start(*tok_group(i), plane=i < 3)
 
-        @pl.when((i > 0) & (i < 5))
+        @pl.when((i > 1) & (i < 5))
         def _():
             cast_forward(*tok_group(i - 1), plane=i < 4)
 
@@ -607,7 +611,6 @@
     up_w,
     down_w,
 ):
-    mig = jnp.concatenate([mig_src, mig_dst, mig_seq])
     rows, width = tokens.shape
     depth, span, units = gate_w.shape[2], down_w.shape[2], down_w.shape[1]
     heads, row_width = queries.shape[1], queries.shape[2]
@@ -616,14 +619,14 @@
     dma = pltpu.SemaphoreType.DMA
     smem = pl.BlockSpec(memory_space=pltpu.SMEM)
     vmem = pl.BlockSpec(memory_space=pltpu.VMEM)
-    hbm = pl.BlockSpec(memory_space=pl.ANY)
+    hbm = pl.BlockSpec(memory_space=pltpu.HBM)
     return pl.pallas_call(
         window_kernel,
         out_shape=(
             jax.ShapeDtypeStruct((queries.shape[0], heads, KV_RANK), bf16),
             jax.ShapeDtypeStruct((rows, width), bf16),
         ),
-        in_specs=[smem] * 3 + [hbm] * 4 + [vmem] * 2 + [hbm] * 3,
+        in_specs=[smem] * 4 + [hbm] * 4 + [vmem] * 2 + [hbm] * 3,
         out_specs=(vmem, vmem),
         scratch_shapes=[
             pltpu.VMEM((LAYERS, PLANE, rows, width), bf16),
@@ -658,12 +661,13 @@
             dma((3,)),
         ],
         compiler_params=pltpu.CompilerParams(
-            collective_id=0, has_side_effects=True, vmem_limit_bytes=58 * 1024 * 1024
+            collective_id=0, has_side_effects=True, vmem_limit_bytes=40 * 1024 * 1024
         ),
     )(
         tables,
         lengths,
-        mig,
+        mig_dst,
+        mig_seq,
         queries,
         pool,
         moved,

time: 64.3 us -> 73.5 us (1.14)
  local copies, waits for them, and re-layouts: 3.09 us -> 12.4 us
  Pallas kernels: 57.8 us -> 58.7 us
    unnamed x2 -> x24, local copies, waits for them, and re-layouts: 3.09 us -> 12.4 us
    pallas_call x1, Pallas kernels: 57.8 us -> 58.7 us  [window(): pl.pallas_call(window_kernel, out_shape=(jax.ShapeDtypeStruct((queries.sh...]
where the time goes in v4:
time: 73.5 us; the launch traced here: 73.1 us
  Pallas kernels  58.7 us (80%)
  local copies, waits for them, and re-layouts  12.4 us (17%)
  between operations  1.95 us (3%)
    pallas_call x1, Pallas kernels, window(): pl.pallas_call(window_kernel, out_shape=(jax.ShapeDtypeStruct((queries.sh...  58.7 us
    unnamed x24, local copies, waits for them, and re-layouts  12.4 us

profile of v4, /device:TPU:0, one launch (start us, length us, event | category | flops | bytes accessed | tf_op | source)
XLA Modules:
  0.0 73.1 jit_solution(11848989940838716065)
XLA Ops:
  1.9 0.0 copy-start
  1.9 1.5 %copy-done = bf16[1,3584,256]{2,1,0:T(8,128)(2,1)S(1)} copy-done((bf16[1,3584,256]{2,1,0:T(8,128)(2,1)S(1)}, bf16[1,3584,256]{2,1,0:T(8,128)(2,1)}, u32[]{:S(2)}) %copy-start) | copy-done | bytes 1835032
  3.4 0.0 copy-start.1
  3.4 1.5 %copy-done.1 = bf16[1,3584,256]{2,1,0:T(8,128)(2,1)S(1)} copy-done((bf16[1,3584,256]{2,1,0:T(8,128)(2,1)S(1)}, bf16[1,3584,256]{2,1,0:T(8,128)(2,1)}, u32[]{:S(2)}) %copy-start.1) | copy-done | bytes 1835032
  4.9 0.0 copy-start.2
  4.9 1.5 %copy-done.2 = bf16[1,2048,448]{1,2,0:T(8,128)(2,1)S(1)} copy-done((bf16[1,2048,448]{1,2,0:T(8,128)(2,1)S(1)}, bf16[1,2048,448]{1,2,0:T(8,128)(2,1)}, u32[]{:S(2)}) %copy-start.2) | copy-done | bytes 1835032
  6.4 0.0 copy-start.3
  6.4 1.2 %copy-done.3 = bf16[6,128,576]{1,2,0:T(8,128)(2,1)S(1)} copy-done((bf16[6,128,576]{1,2,0:T(8,128)(2,1)S(1)}, bf16[6,128,576]{1,2,0:T(8,128)(2,1)}, u32[]{:S(2)}) %copy-start.3) | copy-done | bytes 884760
  7.6 0.0 copy-start.4
  7.6 1.0 %copy-done.4 = bf16[2,128,576]{1,2,0:T(8,128)(2,1)S(1)} copy-done((bf16[2,128,576]{1,2,0:T(8,128)(2,1)S(1)}, bf16[2,128,576]{1,2,0:T(8,128)(2,1)}, u32[]{:S(2)}) %copy-start.4) | copy-done | bytes 294936
  8.6 0.0 copy-start.5
  8.6 0.9 %copy-done.5 = bf16[3,32,576]{2,1,0:T(8,128)(2,1)S(1)} copy-done((bf16[3,32,576]{2,1,0:T(8,128)(2,1)S(1)}, bf16[3,32,576]{2,1,0:T(8,128)(2,1)}, u32[]{:S(2)}) %copy-start.5) | copy-done | bytes 110616
  9.5 0.0 copy-start.6
  9.5 0.9 %copy-done.6 = bf16[16,3584]{1,0:T(8,128)(2,1)S(1)} copy-done((bf16[16,3584]{1,0:T(8,128)(2,1)S(1)}, bf16[16,3584]{1,0:T(8,128)(2,1)}, u32[]{:S(2)}) %copy-start.6) | copy-done | bytes 114712
  10.4 0.0 copy-start.7
  10.4 0.7 copy-done.7
  11.0 0.0 copy-start.8
  11.0 0.7 copy-done.8
  11.7 0.0 copy-start.9
  11.7 0.7 copy-done.9
  12.4 0.0 copy-start.10
  12.4 0.7 copy-done.10
  13.0 58.7 %shard_map.140 = (bf16[3,32,512]{2,1,0:T(8,128)(2,1)S(1)}, bf16[16,3584]{1,0:T(8,128)(2,1)S(1)}) custom-call(s32[1,6]{1,0:T(1,128)S(1)} %copy-done.9, s32[1,1,3]{2,1,0:T(1,128)S(1)} %copy-done.10, s32[1]{0:T(128)S(6)} %copy.17.mig_dst_ref, s32[1]{0:T(128)S(6)} %copy.18.mig_seq_ref, bf16[3,32,576]{2,1,0:T(8,128)(2,1)S(1)} %copy-done.5, ...), custom_call_target="tpu_custom_call" | custom-call | tf_op jit(solution)/shard_map/pallas_call | solution.py:623
  71.8 0.6 copy.19
  72.4 0.6 copy.20
Async XLA Ops:
  1.9 1.5 %copy-start = (bf16[1,3584,256]{2,1,0:T(8,128)(2,1)S(1)}, bf16[1,3584,256]{2,1,0:T(8,128)(2,1)}, u32[]{:S(2)}) copy-start(bf16[1,3584,256]{2,1,0:T(8,128)(2,1)} %gate_w_ref.1) | copy-start | bytes 5505028
  3.4 1.5 %copy-start.1 = (bf16[1,3584,256]{2,1,0:T(8,128)(2,1)S(1)}, bf16[1,3584,256]{2,1,0:T(8,128)(2,1)}, u32[]{:S(2)}) copy-start(bf16[1,3584,256]{2,1,0:T(8,128)(2,1)} %up_w_ref.1) | copy-start | bytes 5505028
  4.9 1.5 %copy-start.2 = (bf16[1,2048,448]{1,2,0:T(8,128)(2,1)S(1)}, bf16[1,2048,448]{1,2,0:T(8,128)(2,1)}, u32[]{:S(2)}) copy-start(bf16[1,2048,448]{1,2,0:T(8,128)(2,1)} %param.26) | copy-start | bytes 5505028
  6.4 1.2 %copy-start.3 = (bf16[6,128,576]{1,2,0:T(8,128)(2,1)S(1)}, bf16[6,128,576]{1,2,0:T(8,128)(2,1)}, u32[]{:S(2)}) copy-start(bf16[6,128,576]{1,2,0:T(8,128)(2,1)} %param.15) | copy-start | bytes 2654212
  7.6 1.0 %copy-start.4 = (bf16[2,128,576]{1,2,0:T(8,128)(2,1)S(1)}, bf16[2,128,576]{1,2,0:T(8,128)(2,1)}, u32[]{:S(2)}) copy-start(bf16[2,128,576]{1,2,0:T(8,128)(2,1)} %param.18) | copy-start | bytes 884740
  8.6 0.9 %copy-start.5 = (bf16[3,32,576]{2,1,0:T(8,128)(2,1)S(1)}, bf16[3,32,576]{2,1,0:T(8,128)(2,1)}, u32[]{:S(2)}) copy-start(bf16[3,32,576]{2,1,0:T(8,128)(2,1)} %queries_ref.1) | copy-start | bytes 331780
  9.5 0.9 %copy-start.6 = (bf16[16,3584]{1,0:T(8,128)(2,1)S(1)}, bf16[16,3584]{1,0:T(8,128)(2,1)}, u32[]{:S(2)}) copy-start(bf16[16,3584]{1,0:T(8,128)(2,1)} %tokens_ref.1) | copy-start | bytes 344068
  10.4 0.7 copy-start.7
  11.0 0.7 copy-start.8
  11.7 0.7 copy-start.9
  12.4 0.7 copy-start.10

commit v5 on v3

--- a/solution.py
+++ b/solution.py
@@ -139,22 +139,20 @@
 def window_kernel(
     tables_ref,
     lengths_ref,
-    mig_ref,
+    mig_dst_ref,
+    mig_seq_ref,
     queries_ref,
     cache_ref,
     pages_ref,
     tokens_ref,
-    routes_ref,
-    gates_ref,
     gate_w_ref,
     up_w_ref,
     down_w_ref,
     attn_ref,
-    moe_ref,
+    ret,
     tok,
     hid,
     out,
-    ret,
     wg,
     wu,
     wd,
@@ -389,11 +387,11 @@
         remote(qry.at[sd], qry.at[sd], qs.at[2], qr.at[2], dev_s).wait_recv()
         local[2].wait()
         page_copy.wait_recv()
-        receives = mig_ref[1] == x
+        receives = mig_dst_ref[0] == x
         lane = lax.broadcasted_iota(jnp.int32, (HEADS_ALL, 128), 1)
         stats = jnp.zeros((HEADS_ALL, 128), jnp.float32)
         for s in range(3):
-            chosen = receives & (mig_ref[2] == s)
+            chosen = receives & (mig_seq_ref[0] == s)
             query = qry[:, s].reshape(HEADS_ALL, KV_RANK + ROPE_DIM)
             pages, masked = [], []
             for j in range(SLOTS):
@@ -467,15 +465,16 @@
             remote(qry.at[dt], qry.at[dt], qs.at[0], qr.at[0], y_dev).wait_recv()
             q_pass.start()
 
-        @pl.when(i == 3)
+        @pl.when(i == 2)
         def _():
             page_copy.start()
-
-        @pl.when(i == 2)
-        def _():
             local[3].wait()
             local[4].wait()
             local[5].wait()
+
+        @pl.when(i == 5)
+        def _():
+            attend()
 
         @pl.when((i > 1) & (i < 6))
         def _():
@@ -494,10 +493,6 @@
             cast_start(*hid_group(i - 2))
 
         @pl.when(i == 6)
-        def _():
-            attend()
-
-        @pl.when(i == 7)
         def _():
             pass_on()
 
@@ -571,6 +566,10 @@
 
     lax.fori_loop(0, 4, out_wait, 0)
     keep.wait()
+
+
+def mix_kernel(raw_ref, ret, routes_ref, gates_ref, attn_ref, moe_ref):
+    attn_ref[...] = raw_ref[...]
     named, scale = routes_ref[...], gates_ref[...]
     count = named.shape[1]
     same = lax.broadcasted_iota(jnp.int32, (count, count), 0) == lax.broadcasted_iota(
@@ -580,7 +579,7 @@
     for e in range(LAYERS):
         hits = jnp.sum(jnp.where(named == e, scale, 0.0), axis=0, keepdims=True)
         coefs.append(jnp.sum(jnp.where(same, hits, 0.0), axis=1, keepdims=True))
-    span = out.shape[3]
+    span = ret.shape[3]
     for p in range(PLANE):
         mixed = coefs[0] * ret[0, p].astype(jnp.float32)
         for e in range(1, LAYERS):
@@ -607,7 +606,6 @@
     up_w,
     down_w,
 ):
-    mig = jnp.concatenate([mig_src, mig_dst, mig_seq])
     rows, width = tokens.shape
     depth, span, units = gate_w.shape[2], down_w.shape[2], down_w.shape[1]
     heads, row_width = queries.shape[1], queries.shape[2]
@@ -617,18 +615,17 @@
     smem = pl.BlockSpec(memory_space=pltpu.SMEM)
     vmem = pl.BlockSpec(memory_space=pltpu.VMEM)
     hbm = pl.BlockSpec(memory_space=pl.ANY)
-    return pl.pallas_call(
+    raw, returned = pl.pallas_call(
         window_kernel,
         out_shape=(
             jax.ShapeDtypeStruct((queries.shape[0], heads, KV_RANK), bf16),
-            jax.ShapeDtypeStruct((rows, width), bf16),
+            jax.ShapeDtypeStruct((LAYERS, PLANE, rows, span), bf16),
         ),
-        in_specs=[smem] * 3 + [hbm] * 4 + [vmem] * 2 + [hbm] * 3,
-        out_specs=(vmem, vmem),
+        in_specs=[smem] * 4 + [hbm] * 7,
+        out_specs=(vmem, hbm),
         scratch_shapes=[
             pltpu.VMEM((LAYERS, PLANE, rows, width), bf16),
             pltpu.VMEM((LAYERS, PLANE, PLANE * rows, depth), bf16),
-            pltpu.VMEM((LAYERS, PLANE, rows, span), bf16),
             pltpu.VMEM((LAYERS, PLANE, rows, span), bf16),
             pltpu.VMEM((width, depth), bf16),
             pltpu.VMEM((width, depth), bf16),
@@ -658,22 +655,31 @@
             dma((3,)),
         ],
         compiler_params=pltpu.CompilerParams(
-            collective_id=0, has_side_effects=True, vmem_limit_bytes=58 * 1024 * 1024
+            collective_id=0, has_side_effects=True, vmem_limit_bytes=60 * 1024 * 1024
         ),
     )(
         tables,
         lengths,
-        mig,
+        mig_dst,
+        mig_seq,
         queries,
         pool,
         moved,
         tokens,
-        routes.T,
-        gates.T,
         gate_w,
         up_w,
         jnp.swapaxes(down_w, 1, 2),
     )
+    return pl.pallas_call(
+        mix_kernel,
+        out_shape=(
+            jax.ShapeDtypeStruct(raw.shape, bf16),
+            jax.ShapeDtypeStruct((rows, width), bf16),
+        ),
+        in_specs=[vmem] * 4,
+        out_specs=(vmem, vmem),
+        compiler_params=pltpu.CompilerParams(vmem_limit_bytes=60 * 1024 * 1024),
+    )(raw, returned, routes.T, gates.T)
 
 
 def solution(mesh):

time: 64.3 us -> 63.6 us (0.989)
  Pallas kernels: 57.8 us -> 61.5 us
  local copies, waits for them, and re-layouts: 3.09 us -> 0 us
  between operations: 2.58 us -> 1.93 us
    unnamed x2 -> x0, local copies, waits for them, and re-layouts: 3.09 us -> none
    pallas_call x0 -> x1, Pallas kernels: none -> 1.93 us  [window(): pl.pallas_call(mix_kernel, out_shape=(jax.ShapeDtypeStruct(raw.shape, bf1...]
    pallas_call x1, Pallas kernels: 57.8 us -> 59.6 us  [window(): pl.pallas_call(window_kernel, out_shape=(jax.ShapeDtypeStruct((queries.sh...]
where the time goes in v5:
time: 63.6 us; the launch traced here: 63.4 us
  Pallas kernels  61.5 us (97%)
  between operations  1.93 us (3%)
    pallas_call x1, Pallas kernels, window(): pl.pallas_call(window_kernel, out_shape=(jax.ShapeDtypeStruct((queries.sh...  59.6 us
    pallas_call x1, Pallas kernels, window(): pl.pallas_call(mix_kernel, out_shape=(jax.ShapeDtypeStruct(raw.shape, bf1...  1.93 us

profile of v5, /device:TPU:0, one launch (start us, length us, event | category | flops | bytes accessed | tf_op | source)
XLA Modules:
  0.0 63.4 jit_solution(17541120281868596946)
XLA Ops:
  1.9 59.6 %shard_map.140 = (bf16[3,32,512]{2,1,0:T(8,128)(2,1)}, bf16[4,8,16,448]{3,2,1,0:T(8,128)(2,1)}) custom-call(s32[1,6]{1,0:T(1,128)} %tables_ref.1, s32[1,1,3]{2,1,0:T(1,128)} %lengths_ref.1, s32[1]{0:T(128)S(6)} %copy.15.mig_dst_ref, s32[1]{0:T(128)S(6)} %copy.16.mig_seq_ref, bf16[3,32,576]{2,1,0:T(8,128)(2,1)} %queries_ref.1, bf16[6,576,128]{2,1,0:T(8,128)(2,1)} %bitcast.6, ...), custom_call_target="tpu_custom_call" | custom-call | tf_op jit(solution)/shard_map/pallas_call | solution.py:618
  61.5 1.9 %shard_map.141 = (bf16[3,32,512]{2,1,0:T(8,128)(2,1)}, bf16[16,3584]{1,0:T(8,128)(2,1)}) custom-call(bf16[3,32,512]{2,1,0:T(8,128)(2,1)} %get-tuple-element.4.raw_ref, bf16[4,8,16,448]{3,2,1,0:T(8,128)(2,1)} %get-tuple-element.5.ret, s32[2,16]{1,0:T(2,128)} %bitcast.8, f32[2,16]{1,0:T(2,128)} %bitcast.9), custom_call_target="tpu_custom_call" | custom-call | tf_op jit(solution)/shard_map/pallas_call | solution.py:673

commit v6 on v5

--- a/solution.py
+++ b/solution.py
@@ -465,16 +465,15 @@
             remote(qry.at[dt], qry.at[dt], qs.at[0], qr.at[0], y_dev).wait_recv()
             q_pass.start()
 
+        @pl.when(i == 3)
+        def _():
+            page_copy.start()
+
         @pl.when(i == 2)
         def _():
-            page_copy.start()
             local[3].wait()
             local[4].wait()
             local[5].wait()
-
-        @pl.when(i == 5)
-        def _():
-            attend()
 
         @pl.when((i > 1) & (i < 6))
         def _():
@@ -493,6 +492,10 @@
             cast_start(*hid_group(i - 2))
 
         @pl.when(i == 6)
+        def _():
+            attend()
+
+        @pl.when(i == 7)
         def _():
             pass_on()
 

time: 63.6 us -> 61.7 us (0.970)
  Pallas kernels: 61.5 us -> 59.6 us
    pallas_call x1, Pallas kernels: 59.6 us -> 57.7 us  [window(): pl.pallas_call(window_kernel, out_shape=(jax.ShapeDtypeStruct((queries.sh...]
where the time goes in v6:
time: 61.7 us; the launch traced here: 61.6 us
  Pallas kernels  59.6 us (97%)
  between operations  1.93 us (3%)
    pallas_call x1, Pallas kernels, window(): pl.pallas_call(window_kernel, out_shape=(jax.ShapeDtypeStruct((queries.sh...  57.7 us
    pallas_call x1, Pallas kernels, window(): pl.pallas_call(mix_kernel, out_shape=(jax.ShapeDtypeStruct(raw.shape, bf1...  1.93 us

profile of v6, /device:TPU:0, one launch (start us, length us, event | category | flops | bytes accessed | tf_op | source)
XLA Modules:
  0.0 61.6 jit_solution(9846797905909466391)
XLA Ops:
  1.9 57.7 %shard_map.140 = (bf16[3,32,512]{2,1,0:T(8,128)(2,1)}, bf16[4,8,16,448]{3,2,1,0:T(8,128)(2,1)}) custom-call(s32[1,6]{1,0:T(1,128)} %tables_ref.1, s32[1,1,3]{2,1,0:T(1,128)} %lengths_ref.1, s32[1]{0:T(128)S(6)} %copy.15.mig_dst_ref, s32[1]{0:T(128)S(6)} %copy.16.mig_seq_ref, bf16[3,32,576]{2,1,0:T(8,128)(2,1)} %queries_ref.1, bf16[6,576,128]{2,1,0:T(8,128)(2,1)} %bitcast.6, ...), custom_call_target="tpu_custom_call" | custom-call | tf_op jit(solution)/shard_map/pallas_call | solution.py:621
  59.6 1.9 %shard_map.141 = (bf16[3,32,512]{2,1,0:T(8,128)(2,1)}, bf16[16,3584]{1,0:T(8,128)(2,1)}) custom-call(bf16[3,32,512]{2,1,0:T(8,128)(2,1)} %get-tuple-element.4.raw_ref, bf16[4,8,16,448]{3,2,1,0:T(8,128)(2,1)} %get-tuple-element.5.ret, s32[2,16]{1,0:T(2,128)} %bitcast.8, f32[2,16]{1,0:T(2,128)} %bitcast.9), custom_call_target="tpu_custom_call" | custom-call | tf_op jit(solution)/shard_map/pallas_call | solution.py:676
